TPU v7x, 32 devices: a whole 2x2x4 slice. The times are simulated.
32 devices in a mesh: cin: 8 (over z, x), cout: 2 (over y), depth: 2 (over core).
Axes of the slice: x: 2, y: 2, z: 4, core: 2. Of those that a mesh axis runs over, the one named last changes fastest.
Arguments:
- features: bfloat16 [8, 512, 4, 128], P(None, 'cin', 'depth'), may hold values from -6 to 6
- kernel: bfloat16 [27, 512, 512], P(None, 'cout', 'cin'), may hold values from -0.0546875 to 0.0546875
- grad_out: bfloat16 [8, 512, 4, 128], P('cin', 'cout', 'depth'), may hold values from -6 to 6
Outputs:
- output: bfloat16 [8, 512, 4, 128], P('cin', 'cout', 'depth')
- input_grad: bfloat16 [8, 512, 4, 128], P('cout', 'cin', 'depth')
- kernel_grad: float32 [27, 512, 512], P(None, 'cout', 'cin')
All inputs are finite; a program needn't handle non-finite values.
Results may differ from a plain program's by a relative error of at most 0.001.
Values may be sent and summed in bfloat16 or wider, within the bound.
No kernel may reach another device: no remote copies, remote signals or barrier semaphores. Data moves between devices by JAX's collectives and lax.ppermute only.
A program may use at most 128 MiB of HBM per device.

v0:
```python
import math
import jax
import jax.numpy as jnp
from jax import lax
from jax.sharding import PartitionSpec as P


def padded_2(x, sides, width):
    for axis, dim in sides:
        size, length = (lax.axis_size(axis), x.shape[dim])
        up = [(i, (i + 1) % size) for i in range(size - 1)]
        down = [(j, i) for i, j in up]
        last = lax.slice_in_dim(x, length - width, length, axis=dim)
        first = lax.slice_in_dim(x, 0, width, axis=dim)
        before = lax.ppermute(last, axis, up)
        after = lax.ppermute(first, axis, down)
        x = jnp.concatenate([before, x, after], axis=dim)
    return x


def conv_rows(padded, weight, count, slab, width):
    total = None
    for depth_off in range(3):
        pieces = [
            padded[
                row_off : row_off + count,
                :,
                depth_off : depth_off + slab,
                col_off : col_off + width,
            ]
            for row_off in range(3)
            for col_off in range(3)
        ]
        stacked = jnp.stack(pieces, axis=1)
        term = jnp.einsum(
            "toc,htcdw->hodw",
            weight[9 * depth_off : 9 * depth_off + 9],
            stacked,
            preferred_element_type=jnp.float32,
        )
        total = term if total is None else total + term
    return total


def weight_terms(padded, grad_own, count, slab, width):
    parts = []
    for depth_off in range(3):
        pieces = [
            padded[
                row_off : row_off + count,
                :,
                depth_off : depth_off + slab,
                col_off : col_off + width,
            ]
            for row_off in range(3)
            for col_off in range(3)
        ]
        stacked = jnp.stack(pieces, axis=1)
        parts.append(
            jnp.einsum("hodw,htcdw->toc", grad_own, stacked, preferred_element_type=jnp.float32)
        )
    return jnp.concatenate(parts, axis=0)


def per_device(features, kernel, grad_out):
    rows_all = features.shape[0]
    slab = features.shape[2]
    width = features.shape[3]
    chan_in = features.shape[1]
    rows_own = rows_all // lax.axis_size("cin")
    slab_ext = padded_2(features, (("depth", 2),), 1)
    feat_pad = jnp.pad(slab_ext, ((1, 1), (0, 0), (0, 0), (1, 1)))
    block = feat_pad
    output = lax.psum_scatter(
        conv_rows(block, kernel, lax.axis_size("cin") * rows_own, slab, width),
        "cin",
        scatter_dimension=0,
        tiled=True,
    ).astype(jnp.bfloat16)
    grad_full = lax.all_gather(grad_out, "cin", axis=0, tiled=True)
    grad_full = padded_2(grad_full, (("depth", 2),), 1)
    grad_pad = jnp.pad(grad_full, ((1, 1), (0, 0), (0, 0), (0, 0)))
    rows_grad = rows_all // lax.axis_size("cout")
    block = grad_pad
    total = jnp.zeros((lax.axis_size("cout") * rows_grad, chan_in, slab, width), jnp.float32)
    for depth_off in range(3):
        part = block[:, :, 2 - depth_off : 2 - depth_off + slab, :]
        mixed = jnp.einsum(
            "toc,hodw->thcdw",
            kernel[9 * depth_off : 9 * depth_off + 9],
            part,
            preferred_element_type=jnp.float32,
        )
        mixed = jnp.pad(mixed, ((0, 0), (0, 0), (0, 0), (0, 0), (1, 1)))
        for row_off in range(3):
            for col_off in range(3):
                total = (
                    total
                    + mixed[
                        3 * row_off + col_off,
                        2 - row_off : 2 - row_off + lax.axis_size("cout") * rows_grad,
                        :,
                        :,
                        2 - col_off : 2 - col_off + width,
                    ]
                )
    input_grad = lax.psum_scatter(total, "cout", scatter_dimension=0, tiled=True).astype(
        jnp.bfloat16
    )
    grad_own = grad_full[:, :, 1 : 1 + slab, :]
    local_terms = weight_terms(feat_pad, grad_own, rows_all, slab, width)
    summed = lax.psum(local_terms, "depth")
    cells = rows_all * slab * lax.axis_size("depth") * width
    kernel_grad = summed * (1.0 / math.sqrt(cells))
    return (output, input_grad, kernel_grad)


def solution(mesh):
    return jax.shard_map(
        per_device,
        mesh=mesh,
        in_specs=(
            P(None, "cin", "depth", None),
            P(None, "cout", "cin"),
            P("cin", "cout", "depth", None),
        ),
        out_specs=(
            P("cin", "cout", "depth", None),
            P("cout", "cin", "depth", None),
            P(None, "cout", "cin"),
        ),
        check_vma=False,
    )
```

profile of v0, /device:TPU:0, one launch (start us, length us, event | category | flops | bytes accessed | tf_op | source)
XLA Modules:
  0.0 189.4 jit_solution(8112478354780090528)
XLA Ops:
  7.2 0.0 all-gather.2.cloned.1.call-start
  7.2 1.0 copy.40
  8.2 2.4 %collective-permute-start = (bf16[8,64,1,128]{3,1,2,0:T(8,128)(2,1)S(1)}, bf16[8,64,1,128]{3,1,2,0:T(8,128)(2,1)S(1)}, u32[]{:S(2)}, u32[]{:S(2)}) collective-permute-start(bf16[8,64,1,128]{3,1,2,0:T(8,128)(2,1)S(1)} %get-tuple-element.25), channel_id=1, source_target_pairs={{0,1},{2,3},{4,5},{6,7},{8,9},{10,11},{12,13},{14,15},{16,17},{18,... | collective-permute-start | bytes 393224 | tf_op jit(solution)/shard_map/ppermute | solution.py:15
  10.6 1.3 collective-permute-start.1
  11.9 1.6 copy.55
  13.5 0.0 all-gather.2.cloned.1.call-update
  13.5 0.0 reduce-scatter.5.cloned.1.call-start
  13.6 0.0 collective-permute-done
  13.6 0.3 collective-permute-done.1
  13.9 0.5 select_maximum_fusion
  14.4 0.7 fusion.85
  15.1 0.8 fusion.95
  15.9 0.9 fusion.94
  16.8 0.9 fusion.93
  17.6 0.8 fusion.92
  18.4 0.9 fusion.84
  19.3 1.0 fusion.83
  20.3 0.9 fusion.82
  21.2 0.8 fusion.91
  22.0 0.0 copy-done.2
  22.0 0.8 bitcast_dynamic-update-slice_fusion
  22.8 0.9 fusion.81
  23.7 0.7 fusion.73
  24.4 0.9 fusion.89
  25.2 0.8 fusion.88
  26.0 0.8 fusion.87
  26.9 0.9 fusion.80
  27.8 0.9 fusion.79
  28.7 28.0 %all-gather.2.cloned.1.call-done = bf16[8,256,2,128]{3,1,2,0:T(8,128)(2,1)} async-done(((bf16[1,256,2,128]{3,1,2,0:T(8,128)(2,1)}), bf16[8,256,2,128]{3,1,2,0:T(8,128)(2,1)}) %all-gather.2.cloned.1.call-update) | async-done | bytes 1048592 | tf_op jit(solution)/shard_map/all_gather | solution.py:80
  56.7 1.4 fusion.104
  58.0 1.3 collective-permute-start.2
  59.4 1.3 collective-permute-start.3
  60.7 0.9 fusion.86
  61.6 1.0 fusion.78
  62.6 0.8 fusion.68
  63.4 0.0 collective-permute-done.2
  63.4 0.0 collective-permute-done.3
  63.4 0.0 copy-done
  63.5 0.4 fusion.5
  63.8 0.8 copy-done.1
  64.6 0.9 convolution_bitcast_fusion.1
  65.5 0.9 convolution_bitcast_fusion.2
  66.5 0.9 convolution_bitcast_fusion
  67.4 3.3 %fusion.54 = f32[8,64,2,128]{3,1,2,0:T(8,128)} fusion(f32[9,10,64,2,128]{4,2,3,1,0:T(8,128)S(1)} %convolution_bitcast_fusion, f32[9,10,64,2,128]{4,2,3,1,0:T(8,128)S(1)} %convolution_bitcast_fusion.1, f32[9,10,64,2,128]{4,2,0,3,1:T(8,128)S(1)} %convolution_bitcast_fusion.2), kind=kLoop, calls=%fused_computation.90 | loop fusion | flops 3407872 | bytes 22937600 | tf_op jit(solution)/shard_map/add | solution.py:98
  70.7 0.0 reduce-scatter.5.cloned.1.call-update
  70.8 0.0 all-reduce.7.cloned.1.call-start
  70.8 2.5 %convolution_bitcast_fusion.3 = f32[9,256,64]{1,2,0:T(8,128)S(1)} fusion(bf16[8,9,64,2,128]{4,2,3,0,1:T(8,128)(2,1)} %fusion.68, bf16[8,256,2,128]{3,1,2,0:T(8,128)(2,1)S(1)} %copy-done), kind=kOutput, calls=%fused_computation.55 | convolution fusion | flops 603979776 | bytes 3997696 | tf_op jit(solution)/shard_map/hodw,htcdw->toc/dot_general | solution.py:60
  73.3 2.5 %convolution_bitcast_fusion.4 = f32[9,256,64]{1,2,0:T(8,128)S(1)} fusion(bf16[8,9,64,2,128]{4,2,3,0,1:T(8,128)(2,1)} %get-tuple-element.9, bf16[8,256,2,128]{3,1,2,0:T(8,128)(2,1)S(1)} %copy-done), kind=kOutput, calls=%fused_computation.56 | convolution fusion | flops 603979776 | bytes 3997696 | tf_op jit(solution)/shard_map/hodw,htcdw->toc/dot_general | solution.py:60
  75.8 2.6 %fusion.19 = f32[9,256,64]{1,2,0:T(8,128)S(1)} fusion(bf16[8,9,64,2,128]{4,2,1,3,0:T(8,128)(2,1)} %fusion.86, bf16[8,256,2,128]{3,1,2,0:T(8,128)(2,1)S(1)} %copy-done), kind=kOutput, calls=%fused_computation.54 | convolution fusion | flops 603979776 | bytes 3997696 | tf_op jit(solution)/shard_map/hodw,htcdw->toc/dot_general | solution.py:60
  78.3 1.4 pad_maximum_fusion
  79.7 0.0 all-reduce.7.cloned.1.call-update
  79.7 0.2 reduce-scatter.3.cloned.1.call-start
  80.0 2.7 %fusion.13 = f32[8,2,128,256,1]{3,2,0,1,4:T(8,128)S(1)} fusion(bf16[8,9,64,2,128]{4,2,3,0,1:T(8,128)(2,1)} %get-tuple-element.9, bf16[27,256,64]{1,2,0:T(8,128)(2,1)S(1)} %copy-done.1), kind=kOutput, calls=%fused_computation.40 | convolution fusion | flops 603979776 | bytes 4751360 | tf_op jit(solution)/shard_map/toc,htcdw->hodw/dot_general | solution.py:35
  82.7 2.7 %fusion.11 = f32[8,2,128,256,1]{3,2,0,1,4:T(8,128)S(1)} fusion(bf16[8,9,64,2,128]{4,2,3,0,1:T(8,128)(2,1)} %fusion.68, bf16[27,256,64]{1,2,0:T(8,128)(2,1)S(1)} %copy-done.1), kind=kOutput, calls=%fused_computation.38 | convolution fusion | flops 603979776 | bytes 4751360 | tf_op jit(solution)/shard_map/toc,htcdw->hodw/dot_general | solution.py:35
  85.5 4.1 %fusion.15 = f32[8,256,2,128]{1,3,2,0:T(8,128)} fusion(f32[8,2,128,256,1]{3,2,0,1,4:T(8,128)S(1)} %fusion.11, f32[8,2,128,256,1]{3,2,0,1,4:T(8,128)S(1)} %fusion.13, bf16[8,9,64,2,128]{4,2,1,3,0:T(8,128)(2,1)} %fusion.86, bf16[27,256,64]{1,2,0:T(8,128)(2,1)S(1)} %copy-done.1), kind=kOutput, calls=%fused_computation.43 | convolution fusion | flops 605028352 | bytes 8945664 | tf_op jit(solution)/shard_map/toc,htcdw->hodw/dot_general | solution.py:35
  89.5 0.0 reduce-scatter.3.cloned.1.call-update
  89.6 0.0 reduce-scatter.5.cloned.1.call-done
  89.6 1.0 convert_element_type.15
  90.6 0.8 copy.73
  91.4 17.4 %all-reduce.7.cloned.1.call-done = f32[27,256,64]{1,2,0:T(8,128)} async-done(((f32[27,256,64]{1,2,0:T(8,128)}), f32[27,256,64]{1,2,0:T(8,128)}) %all-reduce.7.cloned.1.call-update) | async-done | bytes 1769488 | tf_op jit(solution)/shard_map/psum | solution.py:112
  108.8 2.9 %broadcast_multiply_fusion = f32[27,256,64]{1,2,0:T(8,128)} fusion(f32[27,256,64]{1,2,0:T(8,128)} %all-reduce.7.cloned.1.call-done), kind=kLoop, calls=%fused_computation.58 | loop fusion | flops 442368 | bytes 3538944 | tf_op jit(solution)/shard_map/mul | solution.py:114
  111.7 69.4 %reduce-scatter.3.cloned.1.call-done = f32[1,256,2,128]{1,3,2,0:T(8,128)} async-done(((f32[8,256,2,128]{1,3,2,0:T(8,128)}), f32[1,256,2,128]{1,3,2,0:T(8,128)}) %reduce-scatter.3.cloned.1.call-update) | async-done | bytes 262160 | tf_op jit(solution)/shard_map/reduce_scatter | solution.py:74
  181.1 1.0 convert_element_type.14
  182.1 0.8 copy.72
  (4 shorter events, 0.0 us)
Async XLA Ops:
  7.2 49.5 %all-gather.2.cloned.1.call-start = ((), (), s32[]{:S(2)}) async-start(), calls=%async_computation.3 | async-start | bytes 1179648 | tf_op jit(solution)/shard_map/all_gather | solution.py:80
  8.2 5.3 %collective-permute-start = (bf16[8,64,1,128]{3,1,2,0:T(8,128)(2,1)S(1)}, bf16[8,64,1,128]{3,1,2,0:T(8,128)(2,1)S(1)}, u32[]{:S(2)}, u32[]{:S(2)}) collective-permute-start(bf16[8,64,1,128]{3,1,2,0:T(8,128)(2,1)S(1)} %get-tuple-element.25), channel_id=1, source_target_pairs={{0,1},{2,3},{4,5},{6,7},{8,9},{10,11},{12,13},{14,15},{16,17},{18,... | collective-permute-start | bytes 393224 | tf_op jit(solution)/shard_map/ppermute | solution.py:15
  10.6 3.2 %collective-permute-start.1 = (bf16[8,64,1,128]{3,1,2,0:T(8,128)(2,1)S(1)}, bf16[8,64,1,128]{3,1,2,0:T(8,128)(2,1)S(1)}, u32[]{:S(2)}, u32[]{:S(2)}) collective-permute-start(bf16[8,64,1,128]{3,1,2,0:T(8,128)(2,1)S(1)} %get-tuple-element.26), channel_id=1, source_target_pairs={{1,0},{3,2},{5,4},{7,6},{9,8},{11,10},{13,12},{15,14},{17,16},{19,... | collective-permute-start | bytes 393224 | tf_op jit(solution)/shard_map/ppermute | solution.py:16
  13.5 76.1 %reduce-scatter.5.cloned.1.call-start = ((), (), s32[]{:S(2)}) async-start(), calls=%async_computation.4 | async-start | bytes 786432 | tf_op jit(solution)/shard_map/reduce_scatter | solution.py:107
  16.8 5.2 %copy-start.2 = (bf16[8,64,2,128]{3,2,1,0:T(2,128)(2,1)S(1)}, bf16[8,64,2,128]{3,2,1,0:T(2,128)(2,1)}, u32[]{:S(2)}) copy-start(bf16[8,64,2,128]{3,2,1,0:T(2,128)(2,1)} %param.3) | copy-start | bytes 786436
  56.7 6.8 %copy-start = (bf16[8,256,2,128]{3,1,2,0:T(8,128)(2,1)S(1)}, bf16[8,256,2,128]{3,1,2,0:T(8,128)(2,1)}, u32[]{:S(2)}) copy-start(bf16[8,256,2,128]{3,1,2,0:T(8,128)(2,1)} %all-gather.2.cloned.1.call-done) | copy-start | bytes 3145732
  58.0 5.4 %collective-permute-start.2 = (bf16[8,256,1,128]{3,1,2,0:T(8,128)(2,1)S(1)}, bf16[8,256,1,128]{3,1,2,0:T(8,128)(2,1)S(1)}, u32[]{:S(2)}, u32[]{:S(2)}) collective-permute-start(bf16[8,256,1,128]{3,1,2,0:T(8,128)(2,1)S(1)} %get-tuple-element.23), channel_id=1, source_target_pairs={{0,1},{2,3},{4,5},{6,7},{8,9},{10,11},{12,13},{14,15},{16,17},{18,... | collective-permute-start | bytes 1572872 | tf_op jit(solution)/shard_map/ppermute | solution.py:15
  59.4 4.1 %collective-permute-start.3 = (bf16[8,256,1,128]{3,1,2,0:T(8,128)(2,1)S(1)}, bf16[8,256,1,128]{3,1,2,0:T(8,128)(2,1)S(1)}, u32[]{:S(2)}, u32[]{:S(2)}) collective-permute-start(bf16[8,256,1,128]{3,1,2,0:T(8,128)(2,1)S(1)} %get-tuple-element.24), channel_id=1, source_target_pairs={{1,0},{3,2},{5,4},{7,6},{9,8},{11,10},{13,12},{15,14},{17,16},{19,... | collective-permute-start | bytes 1572872 | tf_op jit(solution)/shard_map/ppermute | solution.py:16
  63.4 1.2 copy-start.1
  70.8 38.1 %all-reduce.7.cloned.1.call-start = ((), (), s32[]{:S(2)}) async-start(), calls=%async_computation.5 | async-start | bytes 3538944 | tf_op jit(solution)/shard_map/psum | solution.py:112
  79.7 101.4 %reduce-scatter.3.cloned.1.call-start = ((), (), s32[]{:S(2)}) async-start(), calls=%async_computation.2 | async-start | bytes 2359296 | tf_op jit(solution)/shard_map/reduce_scatter | solution.py:74
Sparse Core Ops, SparseCore 0:
  13.6 42.9 all-gather.1
  70.9 14.0 reduce-scatter.4
  88.1 20.6 all-reduce.6
  112.2 68.8 reduce-scatter.2
where the time goes:
time: 190 us; the launch traced here: 189 us
  waiting for transfers between devices  115 us (61%)
  local copies, waits for them, and re-layouts  21.9 us (12%)
  matrix products  19.9 us (10%)
  between operations  13.9 us (7%)
  other arithmetic  11.9 us (6%)
  starting transfers between devices  6.61 us (3%)
    reduce_scatter x1, waiting for transfers between devices, per_device(): lax.psum_scatter(conv_rows(block, kernel, lax.axis_size('cin') * rows_own...  69.4 us
    all_gather x1, waiting for transfers between devices, per_device(): grad_full = lax.all_gather(grad_out, 'cin', axis=0, tiled=True)  28 us
    unnamed x25, local copies, waits for them, and re-layouts  17.7 us
    psum x1, waiting for transfers between devices, per_device(): summed = lax.psum(local_terms, 'depth')  17.4 us
    dot_general x3, matrix products, conv_rows(): jnp.einsum('toc,htcdw->hodw', weight[9 * depth_off:9 * depth_off + 9], st...  9.56 us
    dot_general x3, matrix products, weight_terms(): jnp.einsum('hodw,htcdw->toc', grad_own, stacked, preferred_element_type=j...  7.5 us
  transfers between devices with their start and end apart: 8, of which 4 were waited for; matrix products, arithmetic and copies ran while one was open for 22% of the time, Pallas kernels for 0%

commit v1 on v0

--- a/solution.py
+++ b/solution.py
@@ -77,7 +77,13 @@
         scatter_dimension=0,
         tiled=True,
     ).astype(jnp.bfloat16)
-    grad_full = lax.all_gather(grad_out, "cin", axis=0, tiled=True)
+    n_dev = lax.axis_size("cin")
+    held, shards = (grad_out, [grad_out])
+    for _ in range(n_dev - 1):
+        held = lax.ppermute(held, "cin", [(i_2, (i_2 + 1) % n_dev) for i_2 in range(n_dev)])
+        shards.insert(0, held)
+    line = jnp.concatenate(shards, axis=0)
+    grad_full = jnp.roll(line, (lax.axis_index("cin") + 1) * grad_out.shape[0], axis=0)
     grad_full = padded_2(grad_full, (("depth", 2),), 1)
     grad_pad = jnp.pad(grad_full, ((1, 1), (0, 0), (0, 0), (0, 0)))
     rows_grad = rows_all // lax.axis_size("cout")

time: 190 us -> 176 us (0.926)
  local copies, waits for them, and re-layouts: 21.9 us -> 11.5 us
  matrix products: 19.9 us -> 11.4 us
  starting transfers between devices: 6.61 us -> 8.96 us
  between operations: 13.9 us -> 16 us
  waiting for transfers between devices: 115 us -> 117 us
    ppermute x0 -> x7, waiting for transfers between devices: none -> 49.8 us  [per_device(): lax.ppermute(held, 'cin', [(i_2, (i_2 + 1) % n_dev) for i_2 in range(n_de...]
    all_gather x1 -> x0, waiting for transfers between devices: 28 us -> none  [per_device(): grad_full = lax.all_gather(grad_out, 'cin', axis=0, tiled=True)]
    reduce_scatter x1, waiting for transfers between devices: 69.4 us -> 57.4 us  [per_device(): lax.psum_scatter(conv_rows(block, kernel, lax.axis_size('cin') * rows_own...]
    psum x1, waiting for transfers between devices: 17.4 us -> 8.79 us  [per_device(): summed = lax.psum(local_terms, 'depth')]
    unnamed x25 -> x56, local copies, waits for them, and re-layouts: 17.7 us -> 10.4 us
    dot_general x3, matrix products: 7.5 us -> 2.42 us  [weight_terms(): jnp.einsum('hodw,htcdw->toc', grad_own, stacked, preferred_element_type=j...]
    dot_general x3, matrix products: 9.56 us -> 6.2 us  [conv_rows(): jnp.einsum('toc,htcdw->hodw', weight[9 * depth_off:9 * depth_off + 9], st...]
    ppermute x0 -> x7, starting transfers between devices: none -> 2.39 us  [per_device(): lax.ppermute(held, 'cin', [(i_2, (i_2 + 1) % n_dev) for i_2 in range(n_de...]
  transfers between devices with their start and end apart: 8 -> 14, of which waited for: 4 -> 10; matrix products, arithmetic and copies ran while one was open for 22% -> 11% of each run, Pallas kernels for 0% -> 0%
where the time goes in v1:
time: 176 us; the launch traced here: 175 us
  waiting for transfers between devices  117 us (66%)
  between operations  16 us (9%)
  local copies, waits for them, and re-layouts  11.5 us (7%)
  matrix products  11.4 us (6%)
  other arithmetic  10.4 us (6%)
  starting transfers between devices  8.96 us (5%)
    reduce_scatter x1, waiting for transfers between devices, per_device(): lax.psum_scatter(conv_rows(block, kernel, lax.axis_size('cin') * rows_own...  57.4 us
    ppermute x7, waiting for transfers between devices, per_device(): lax.ppermute(held, 'cin', [(i_2, (i_2 + 1) % n_dev) for i_2 in range(n_de...  49.8 us
    unnamed x56, local copies, waits for them, and re-layouts  10.4 us
    psum x1, waiting for transfers between devices, per_device(): summed = lax.psum(local_terms, 'depth')  8.79 us
    dot_general x3, matrix products, conv_rows(): jnp.einsum('toc,htcdw->hodw', weight[9 * depth_off:9 * depth_off + 9], st...  6.2 us
    ppermute x2, starting transfers between devices, padded_2(): before = lax.ppermute(last, axis, up)  3.69 us
  transfers between devices with their start and end apart: 14, of which 10 were waited for; matrix products, arithmetic and copies ran while one was open for 11% of the time, Pallas kernels for 0%

profile of v1, /device:TPU:0, one launch (start us, length us, event | category | flops | bytes accessed | tf_op | source)
XLA Modules:
  0.0 175.1 jit_solution(4281684894889445763)
XLA Ops:
  8.0 0.0 reduce-scatter.5.cloned.1.call-start
  8.0 1.0 copy.6
  9.1 2.4 %collective-permute-start = (bf16[8,64,1,128]{3,1,2,0:T(8,128)(2,1)S(1)}, bf16[8,64,1,128]{3,1,2,0:T(8,128)(2,1)S(1)}, u32[]{:S(2)}, u32[]{:S(2)}) collective-permute-start(bf16[8,64,1,128]{3,1,2,0:T(8,128)(2,1)S(1)} %get-tuple-element.22), channel_id=1, source_target_pairs={{0,1},{2,3},{4,5},{6,7},{8,9},{10,11},{12,13},{14,15},{16,17},{18,... | collective-permute-start | bytes 393224 | tf_op jit(solution)/shard_map/ppermute | solution.py:15
  11.4 1.3 collective-permute-start.1
  12.7 0.9 copy.21
  13.7 2.4 %collective-permute-start.2 = (bf16[1,256,2,128]{3,1,2,0:T(8,128)(2,1)S(1)}, bf16[1,256,2,128]{3,1,2,0:T(8,128)(2,1)S(1)}, u32[]{:S(2)}, u32[]{:S(2)}) collective-permute-start(bf16[1,256,2,128]{3,1,2,0:T(8,128)(2,1)S(1)} %copy.21), channel_id=1, source_target_pairs={{0,4},{4,8},{8,12},{12,16},{16,20},{20,24},{24,28},{28,0},{1,5},{5... | collective-permute-start | bytes 393224 | tf_op jit(solution)/shard_map/ppermute | solution.py:83
  16.1 0.5 select_maximum_fusion
  16.7 0.2 fusion.84
  16.9 0.4 fusion.83
  17.3 0.3 fusion.82
  17.6 0.1 bitcast_dynamic-update-slice_fusion
  17.6 0.2 fusion.81
  17.9 0.2 fusion.80
  18.2 0.2 fusion.79
  18.4 0.4 fusion.78
  18.9 4.2 %collective-permute-done.2 = bf16[1,256,2,128]{3,1,2,0:T(8,128)(2,1)S(1)} collective-permute-done((bf16[1,256,2,128]{3,1,2,0:T(8,128)(2,1)S(1)}, bf16[1,256,2,128]{3,1,2,0:T(8,128)(2,1)S(1)}, u32[]{:S(2)}, u32[]{:S(2)}) %collective-permute-start.2) | collective-permute-done | bytes 131104 | tf_op jit(solution)/shard_map/ppermute | solution.py:83
  23.1 0.2 fusion.94
  23.3 8.1 %collective-permute-done.3 = bf16[1,256,2,128]{3,1,2,0:T(8,128)(2,1)S(1)} collective-permute-done((bf16[1,256,2,128]{3,1,2,0:T(8,128)(2,1)S(1)}, bf16[1,256,2,128]{3,1,2,0:T(8,128)(2,1)S(1)}, u32[]{:S(2)}, u32[]{:S(2)}) %collective-permute-start.3) | collective-permute-done | bytes 131104 | tf_op jit(solution)/shard_map/ppermute | solution.py:83
  31.4 0.2 fusion.93
  31.6 7.5 %collective-permute-done.4 = bf16[1,256,2,128]{3,1,2,0:T(8,128)(2,1)S(1)} collective-permute-done((bf16[1,256,2,128]{3,1,2,0:T(8,128)(2,1)S(1)}, bf16[1,256,2,128]{3,1,2,0:T(8,128)(2,1)S(1)}, u32[]{:S(2)}, u32[]{:S(2)}) %collective-permute-start.4) | collective-permute-done | bytes 131104 | tf_op jit(solution)/shard_map/ppermute | solution.py:83
  39.0 0.1 fusion.92
  39.1 7.5 %collective-permute-done.5 = bf16[1,256,2,128]{3,1,2,0:T(8,128)(2,1)S(1)} collective-permute-done((bf16[1,256,2,128]{3,1,2,0:T(8,128)(2,1)S(1)}, bf16[1,256,2,128]{3,1,2,0:T(8,128)(2,1)S(1)}, u32[]{:S(2)}, u32[]{:S(2)}) %collective-permute-start.5) | collective-permute-done | bytes 131104 | tf_op jit(solution)/shard_map/ppermute | solution.py:83
  46.7 0.2 fusion.89
  46.9 7.5 %collective-permute-done.6 = bf16[1,256,2,128]{3,1,2,0:T(8,128)(2,1)S(1)} collective-permute-done((bf16[1,256,2,128]{3,1,2,0:T(8,128)(2,1)S(1)}, bf16[1,256,2,128]{3,1,2,0:T(8,128)(2,1)S(1)}, u32[]{:S(2)}, u32[]{:S(2)}) %collective-permute-start.6) | collective-permute-done | bytes 131104 | tf_op jit(solution)/shard_map/ppermute | solution.py:83
  54.4 0.1 fusion.88
  54.4 7.6 %collective-permute-done.7 = bf16[1,256,2,128]{3,1,2,0:T(8,128)(2,1)S(1)} collective-permute-done((bf16[1,256,2,128]{3,1,2,0:T(8,128)(2,1)S(1)}, bf16[1,256,2,128]{3,1,2,0:T(8,128)(2,1)S(1)}, u32[]{:S(2)}, u32[]{:S(2)}) %collective-permute-start.7) | collective-permute-done | bytes 131104 | tf_op jit(solution)/shard_map/ppermute | solution.py:83
  62.0 0.2 fusion.87
  62.2 7.5 %collective-permute-done.8 = bf16[1,256,2,128]{3,1,2,0:T(8,128)(2,1)S(1)} collective-permute-done((bf16[1,256,2,128]{3,1,2,0:T(8,128)(2,1)S(1)}, bf16[1,256,2,128]{3,1,2,0:T(8,128)(2,1)S(1)}, u32[]{:S(2)}, u32[]{:S(2)}) %collective-permute-start.8) | collective-permute-done | bytes 131104 | tf_op jit(solution)/shard_map/ppermute | solution.py:83
  70.2 0.1 constant_dynamic-slice_fusion.1
  70.3 1.3 collective-permute-start.9
  71.6 1.3 collective-permute-start.10
  72.9 0.2 fusion.86
  73.1 0.2 fusion.68
  73.3 0.1 constant_dynamic-slice_fusion.2
  73.4 1.1 copy-done.2
  74.5 0.9 collective-permute-done.10
  75.4 0.3 fusion.5
  75.7 0.9 convolution_bitcast_fusion.1
  76.7 0.9 convolution_bitcast_fusion.2
  77.6 0.9 convolution_bitcast_fusion
  78.6 3.3 %fusion.54 = f32[8,64,2,128]{3,1,2,0:T(8,128)} fusion(f32[9,10,64,2,128]{4,2,3,1,0:T(8,128)S(1)} %convolution_bitcast_fusion, f32[9,10,64,2,128]{4,2,3,1,0:T(8,128)S(1)} %convolution_bitcast_fusion.1, f32[9,10,64,2,128]{4,2,0,3,1:T(8,128)S(1)} %convolution_bitcast_fusion.2), kind=kLoop, calls=%fused_computation.90 | loop fusion | flops 3407872 | bytes 22937600 | tf_op jit(solution)/shard_map/add | solution.py:104
  81.8 0.0 reduce-scatter.5.cloned.1.call-update
  81.9 0.2 all-reduce.7.cloned.1.call-start
  82.1 0.8 convolution_bitcast_fusion.3
  82.9 0.8 copy-done.1
  83.8 0.8 convolution_bitcast_fusion.4
  84.6 0.2 copy-done.3
  84.8 0.6 copy-done.8
  85.4 0.8 fusion.19
  86.2 1.4 pad_maximum_fusion
  87.6 0.0 all-reduce.7.cloned.1.call-update
  87.6 0.0 reduce-scatter.3.cloned.1.call-start
  87.7 2.7 %fusion.13 = f32[8,2,128,256,1]{3,2,0,1,4:T(8,128)S(1)} fusion(bf16[8,9,64,2,128]{4,2,3,0,1:T(8,128)(2,1)} %copy-done, bf16[27,256,64]{1,2,0:T(8,128)(2,1)S(1)} %copy-done.6), kind=kOutput, calls=%fused_computation.40 | convolution fusion | flops 603979776 | bytes 4751360 | tf_op jit(solution)/shard_map/toc,htcdw->hodw/dot_general | solution.py:35
  90.4 1.0 fusion.11
  91.5 1.2 copy-done.4
  92.7 2.4 %fusion.15 = f32[8,256,2,128]{1,3,2,0:T(8,128)} fusion(f32[8,2,128,256,1]{3,2,0,1,4:T(8,128)S(1)} %fusion.11, f32[8,2,128,256,1]{3,2,0,1,4:T(8,128)S(1)} %fusion.13, bf16[8,9,64,2,128]{4,2,1,3,0:T(8,128)(2,1)S(1)} %copy-done.4, bf16[27,256,64]{1,2,0:T(8,128)(2,1)S(1)} %copy-done.6), kind=kOutput, calls=%fused_computation.43 | convolution fusion | flops 605028352 | bytes 8945664 | tf_op jit(solution)/shard_map/toc,htcdw->hodw/dot_general | solution.py:35
  95.1 0.0 reduce-scatter.5.cloned.1.call-done
  95.2 1.0 convert_element_type.15
  96.1 0.8 copy.41
  96.9 8.8 %all-reduce.7.cloned.1.call-done = f32[27,256,64]{1,2,0:T(8,128)} async-done(((f32[27,256,64]{1,2,0:T(8,128)}), f32[27,256,64]{1,2,0:T(8,128)}) %all-reduce.7.cloned.1.call-update) | async-done | bytes 1769488 | tf_op jit(solution)/shard_map/psum | solution.py:118
  105.7 2.9 %broadcast_multiply_fusion = f32[27,256,64]{1,2,0:T(8,128)} fusion(f32[27,256,64]{1,2,0:T(8,128)} %all-reduce.7.cloned.1.call-done), kind=kLoop, calls=%fused_computation.58 | loop fusion | flops 442368 | bytes 3538944 | tf_op jit(solution)/shard_map/mul | solution.py:120
  108.6 57.4 %reduce-scatter.3.cloned.1.call-done = f32[1,256,2,128]{1,3,2,0:T(8,128)} async-done(((f32[8,256,2,128]{1,3,2,0:T(8,128)}), f32[1,256,2,128]{1,3,2,0:T(8,128)}) %reduce-scatter.3.cloned.1.call-update) | async-done | bytes 262160 | tf_op jit(solution)/shard_map/reduce_scatter | solution.py:74
  165.9 1.0 convert_element_type.14
  166.9 0.8 copy.40
  (48 shorter events, 0.6 us)
Async XLA Ops:
  8.0 87.1 %reduce-scatter.5.cloned.1.call-start = ((), (), s32[]{:S(2)}) async-start(), calls=%async_computation.3 | async-start | bytes 786432 | tf_op jit(solution)/shard_map/reduce_scatter | solution.py:113
  9.1 7.0 %collective-permute-start = (bf16[8,64,1,128]{3,1,2,0:T(8,128)(2,1)S(1)}, bf16[8,64,1,128]{3,1,2,0:T(8,128)(2,1)S(1)}, u32[]{:S(2)}, u32[]{:S(2)}) collective-permute-start(bf16[8,64,1,128]{3,1,2,0:T(8,128)(2,1)S(1)} %get-tuple-element.22), channel_id=1, source_target_pairs={{0,1},{2,3},{4,5},{6,7},{8,9},{10,11},{12,13},{14,15},{16,17},{18,... | collective-permute-start | bytes 393224 | tf_op jit(solution)/shard_map/ppermute | solution.py:15
  11.4 4.6 %collective-permute-start.1 = (bf16[8,64,1,128]{3,1,2,0:T(8,128)(2,1)S(1)}, bf16[8,64,1,128]{3,1,2,0:T(8,128)(2,1)S(1)}, u32[]{:S(2)}, u32[]{:S(2)}) collective-permute-start(bf16[8,64,1,128]{3,1,2,0:T(8,128)(2,1)S(1)} %get-tuple-element.23), channel_id=1, source_target_pairs={{1,0},{3,2},{5,4},{7,6},{9,8},{11,10},{13,12},{15,14},{17,16},{19,... | collective-permute-start | bytes 393224 | tf_op jit(solution)/shard_map/ppermute | solution.py:16
  13.7 9.4 %collective-permute-start.2 = (bf16[1,256,2,128]{3,1,2,0:T(8,128)(2,1)S(1)}, bf16[1,256,2,128]{3,1,2,0:T(8,128)(2,1)S(1)}, u32[]{:S(2)}, u32[]{:S(2)}) collective-permute-start(bf16[1,256,2,128]{3,1,2,0:T(8,128)(2,1)S(1)} %copy.21), channel_id=1, source_target_pairs={{0,4},{4,8},{8,12},{12,16},{16,20},{20,24},{24,28},{28,0},{1,5},{5... | collective-permute-start | bytes 393224 | tf_op jit(solution)/shard_map/ppermute | solution.py:83
  16.0 1.5 copy-start.10
  18.9 50.9 %copy-start = (bf16[8,9,64,2,128]{4,2,3,0,1:T(8,128)(2,1)}, bf16[8,9,64,2,128]{4,2,3,0,1:T(8,128)(2,1)S(1)}, u32[]{:S(2)}) copy-start(bf16[8,9,64,2,128]{4,2,3,0,1:T(8,128)(2,1)S(1)} %get-tuple-element.8) | copy-start | bytes 7077892
  23.1 8.3 %collective-permute-start.3 = (bf16[1,256,2,128]{3,1,2,0:T(8,128)(2,1)S(1)}, bf16[1,256,2,128]{3,1,2,0:T(8,128)(2,1)S(1)}, u32[]{:S(2)}, u32[]{:S(2)}) collective-permute-start(bf16[1,256,2,128]{3,1,2,0:T(8,128)(2,1)S(1)} %collective-permute-done.2), channel_id=1, source_target_pairs={{0,4},{4,8},{8,12},{12,16},{16,20},{20,24},{24,28},{28,0},{1,5},{5... | collective-permute-start | bytes 393224 | tf_op jit(solution)/shard_map/ppermute | solution.py:83
  31.4 7.7 %collective-permute-start.4 = (bf16[1,256,2,128]{3,1,2,0:T(8,128)(2,1)S(1)}, bf16[1,256,2,128]{3,1,2,0:T(8,128)(2,1)S(1)}, u32[]{:S(2)}, u32[]{:S(2)}) collective-permute-start(bf16[1,256,2,128]{3,1,2,0:T(8,128)(2,1)S(1)} %collective-permute-done.3), channel_id=1, source_target_pairs={{0,4},{4,8},{8,12},{12,16},{16,20},{20,24},{24,28},{28,0},{1,5},{5... | collective-permute-start | bytes 393224 | tf_op jit(solution)/shard_map/ppermute | solution.py:83
  31.6 38.3 %copy-start.9 = (bf16[1,256,2,128]{3,2,1,0:T(2,128)(2,1)S(1)}, bf16[1,256,2,128]{3,2,1,0:T(2,128)(2,1)}, u32[]{:S(2)}) copy-start(bf16[1,256,2,128]{3,2,1,0:T(2,128)(2,1)} %param.5) | copy-start | bytes 393220
  39.0 7.7 %collective-permute-start.5 = (bf16[1,256,2,128]{3,1,2,0:T(8,128)(2,1)S(1)}, bf16[1,256,2,128]{3,1,2,0:T(8,128)(2,1)S(1)}, u32[]{:S(2)}, u32[]{:S(2)}) collective-permute-start(bf16[1,256,2,128]{3,1,2,0:T(8,128)(2,1)S(1)} %collective-permute-done.4), channel_id=1, source_target_pairs={{0,4},{4,8},{8,12},{12,16},{16,20},{20,24},{24,28},{28,0},{1,5},{5... | collective-permute-start | bytes 393224 | tf_op jit(solution)/shard_map/ppermute | solution.py:83
  46.7 7.7 %collective-permute-start.6 = (bf16[1,256,2,128]{3,1,2,0:T(8,128)(2,1)S(1)}, bf16[1,256,2,128]{3,1,2,0:T(8,128)(2,1)S(1)}, u32[]{:S(2)}, u32[]{:S(2)}) collective-permute-start(bf16[1,256,2,128]{3,1,2,0:T(8,128)(2,1)S(1)} %collective-permute-done.5), channel_id=1, source_target_pairs={{0,4},{4,8},{8,12},{12,16},{16,20},{20,24},{24,28},{28,0},{1,5},{5... | collective-permute-start | bytes 393224 | tf_op jit(solution)/shard_map/ppermute | solution.py:83
  54.4 7.7 %collective-permute-start.7 = (bf16[1,256,2,128]{3,1,2,0:T(8,128)(2,1)S(1)}, bf16[1,256,2,128]{3,1,2,0:T(8,128)(2,1)S(1)}, u32[]{:S(2)}, u32[]{:S(2)}) collective-permute-start(bf16[1,256,2,128]{3,1,2,0:T(8,128)(2,1)S(1)} %collective-permute-done.6), channel_id=1, source_target_pairs={{0,4},{4,8},{8,12},{12,16},{16,20},{20,24},{24,28},{28,0},{1,5},{5... | collective-permute-start | bytes 393224 | tf_op jit(solution)/shard_map/ppermute | solution.py:83
  62.0 7.7 %collective-permute-start.8 = (bf16[1,256,2,128]{3,1,2,0:T(8,128)(2,1)S(1)}, bf16[1,256,2,128]{3,1,2,0:T(8,128)(2,1)S(1)}, u32[]{:S(2)}, u32[]{:S(2)}) collective-permute-start(bf16[1,256,2,128]{3,1,2,0:T(8,128)(2,1)S(1)} %collective-permute-done.7), channel_id=1, source_target_pairs={{0,4},{4,8},{8,12},{12,16},{16,20},{20,24},{24,28},{28,0},{1,5},{5... | collective-permute-start | bytes 393224 | tf_op jit(solution)/shard_map/ppermute | solution.py:83
  70.2 3.2 %copy-start.7 = (bf16[16,256,2,128]{3,1,2,0:T(8,128)(2,1)}, bf16[16,256,2,128]{3,1,2,0:T(8,128)(2,1)S(1)}, u32[]{:S(2)}) copy-start(bf16[16,256,2,128]{3,1,2,0:T(8,128)(2,1)S(1)} %constant_dynamic-update-slice_fusion) | copy-start | bytes 6291460
  70.3 3.2 %collective-permute-start.9 = (bf16[8,256,1,128]{3,1,2,0:T(8,128)(2,1)S(1)}, bf16[8,256,1,128]{3,1,2,0:T(8,128)(2,1)S(1)}, u32[]{:S(2)}, u32[]{:S(2)}) collective-permute-start(bf16[8,256,1,128]{3,1,2,0:T(8,128)(2,1)S(1)} %get-tuple-element.6), channel_id=1, source_target_pairs={{0,1},{2,3},{4,5},{6,7},{8,9},{10,11},{12,13},{14,15},{16,17},{18,... | collective-permute-start | bytes 1572872 | tf_op jit(solution)/shard_map/ppermute | solution.py:15
  71.6 3.8 %collective-permute-start.10 = (bf16[8,256,1,128]{3,1,2,0:T(8,128)(2,1)S(1)}, bf16[8,256,1,128]{3,1,2,0:T(8,128)(2,1)S(1)}, u32[]{:S(2)}, u32[]{:S(2)}) collective-permute-start(bf16[8,256,1,128]{3,1,2,0:T(8,128)(2,1)S(1)} %get-tuple-element.7), channel_id=1, source_target_pairs={{1,0},{3,2},{5,4},{7,6},{9,8},{11,10},{13,12},{15,14},{17,16},{19,... | collective-permute-start | bytes 1572872 | tf_op jit(solution)/shard_map/ppermute | solution.py:16
  73.1 1.5 copy-start.2
  73.4 2.3 %copy-start.5 = (bf16[27,256,64]{1,2,0:T(8,128)(2,1)S(1)}, bf16[27,256,64]{1,2,0:T(8,128)(2,1)}, u32[]{:S(2)}) copy-start(bf16[27,256,64]{1,2,0:T(8,128)(2,1)} %param.4) | copy-start | bytes 2654212
  81.9 23.8 %all-reduce.7.cloned.1.call-start = ((), (), s32[]{:S(2)}) async-start(), calls=%async_computation.4 | async-start | bytes 3538944 | tf_op jit(solution)/shard_map/psum | solution.py:118
  82.1 1.7 copy-start.1
  82.9 1.8 %copy-start.3 = (bf16[8,9,64,2,128]{4,2,1,3,0:T(8,128)(2,1)S(1)}, bf16[8,9,64,2,128]{4,2,1,3,0:T(8,128)(2,1)}, u32[]{:S(2)}) copy-start(bf16[8,9,64,2,128]{4,2,1,3,0:T(8,128)(2,1)} %copy-done.2) | copy-start | bytes 7077892
  82.9 2.5 %copy-start.8 = (bf16[16,256,2,128]{3,1,2,0:T(8,128)(2,1)S(1)}, bf16[16,256,2,128]{3,1,2,0:T(8,128)(2,1)}, u32[]{:S(2)}) copy-start(bf16[16,256,2,128]{3,1,2,0:T(8,128)(2,1)} %copy-done.7) | copy-start | bytes 6291460
  86.2 1.5 copy-start.6
  87.6 78.3 %reduce-scatter.3.cloned.1.call-start = ((), (), s32[]{:S(2)}) async-start(), calls=%async_computation.2 | async-start | bytes 2359296 | tf_op jit(solution)/shard_map/reduce_scatter | solution.py:74
  90.4 2.2 %copy-start.4 = (bf16[8,9,64,2,128]{4,2,1,3,0:T(8,128)(2,1)S(1)}, bf16[8,9,64,2,128]{4,2,1,3,0:T(8,128)(2,1)}, u32[]{:S(2)}) copy-start(bf16[8,9,64,2,128]{4,2,1,3,0:T(8,128)(2,1)} %copy-done.2) | copy-start | bytes 7077892
Sparse Core Ops, SparseCore 0:
  82.0 12.2 reduce-scatter.4
  98.2 67.6 reduce-scatter.2
Sparse Core Ops, SparseCore 1:
  87.7 17.9 all-reduce.6
